TPU v7x, 32 devices: a whole 2x2x4 slice. The times are simulated.
32 devices in a mesh: groups: 2 (over y), ctx: 4 (over z), head: 2 (over x), rep: 2 (over core).
Axes of the slice: x: 2, y: 2, z: 4, core: 2. Of those that a mesh axis runs over, the one named last changes fastest.
Arguments:
- queries: bfloat16 [1024, 5120], P(('groups', 'ctx'), 'head'), parts along dimension 0, may hold values from -50 to 50
- key_vectors: bfloat16 [1024, 5120], P(('groups', 'ctx'), 'head'), parts along dimension 0, may hold values from -5 to 5
- values: bfloat16 [1024, 5120], P(('groups', 'ctx'), 'head'), parts along dimension 0, may hold values from -6 to 6
- learn_rates: float32 [8, 1024], P('head', ('groups', 'ctx')), parts along dimension 1, may hold values from 0.02 to 0.2
- fast_weights: float32 [16, 3, 640, 640], P(('groups', 'head'), None, ('ctx', 'rep')), parts along dimension 0, may hold values from -0.25 to 0.25
- momentum: float32 [16, 3, 640, 640], P(('groups', 'head'), None, ('ctx', 'rep')), parts along dimension 0, may hold values from -0.25 to 0.25
Outputs:
- layer_output: bfloat16 [1024, 5120], P(('groups', 'ctx'), ('head', 'rep')), parts along dimension 0
- fast_updated: float32 [16, 3, 640, 640], P(('groups', 'head'), None, ('ctx', 'rep')), parts along dimension 0
There are 2 independent parts, one for each index of `groups`. A program takes and returns all parts, laid end to end along the dimension named above; each array names one. Nothing has to cross between parts.
All inputs are finite; a program needn't handle non-finite values.
Results may differ from a plain program's by a relative error of at most 0.038.
Values may be sent and summed in bfloat16 or wider, within the bound.
A program may use at most 64 MiB of HBM per device.

v0:
```python
import jax
import jax.numpy as jnp
from jax import lax
from jax.sharding import PartitionSpec as P

epsilon = 1e-06
momentum_decay = 0.9


def passed_along(value, axis, steps):
    count = lax.axis_size(axis)
    initial, last = (max(0, -steps), min(count, count - steps))
    return lax.ppermute(value, axis, [(source, source + steps) for source in range(initial, last)])


def unit_rows(tensor):
    widened = tensor.astype(jnp.float32)
    factor = lax.rsqrt(jnp.mean(widened * widened, axis=-1, keepdims=True) + epsilon)
    return (widened * factor).astype(jnp.bfloat16)


def swiglu_apply(inputs, weights):
    gate = jnp.einsum("thd,hrd->htr", inputs, weights[:, 0], preferred_element_type=jnp.float32)
    upward = jnp.einsum("thd,hrd->htr", inputs, weights[:, 1], preferred_element_type=jnp.float32)
    hidden = (jax.nn.silu(gate) * upward).astype(jnp.bfloat16)
    return jnp.einsum("htr,hrd->htd", hidden, weights[:, 2], preferred_element_type=jnp.float32)


def window_attention(query_own, key_own, value_own, key_prior, value_prior, first_block):
    tok_rows = query_own.shape[0]
    per_rep = query_own.shape[1]
    width = query_own.shape[2]
    block_rows = min(tok_rows, 512)
    block_count = tok_rows // block_rows
    key_window = jnp.concatenate([key_prior, key_own], axis=0)
    value_window = jnp.concatenate([value_prior, value_own], axis=0)
    score_scale = width ** (-0.5)
    position = jnp.arange(2 * tok_rows)
    valid = jnp.logical_or(position >= tok_rows, jnp.logical_not(first_block))
    query_blocks = query_own.reshape(block_count, block_rows, per_rep, width)

    def one_block(query_block):
        scores = (
            jnp.einsum("tad,sad->ats", query_block, key_window, preferred_element_type=jnp.float32)
            * score_scale
        )
        scores = jnp.where(valid[None, None, :], scores, -jnp.inf)
        peak = jnp.max(scores, axis=-1, keepdims=True)
        weights = jnp.exp(scores - peak)
        probs = (weights / jnp.sum(weights, axis=-1, keepdims=True)).astype(jnp.bfloat16)
        return jnp.einsum("ats,sad->tad", probs, value_window, preferred_element_type=jnp.float32)

    return lax.map(one_block, query_blocks).reshape(tok_rows, per_rep, width)


def on_device(queries, key_vectors, values, learn_rates, fast_weights, momentum):
    tok_rows = queries.shape[0]
    head_count = fast_weights.shape[0]
    width = fast_weights.shape[3]
    rep_count = lax.axis_size("rep")
    per_rep = head_count // rep_count
    rep_index = lax.axis_index("rep")
    ctx_index = lax.axis_index("ctx")
    total_tokens = tok_rows * lax.axis_size("ctx")
    query_heads = queries.reshape(tok_rows, head_count, width)
    key_heads = key_vectors.reshape(tok_rows, head_count, width)
    value_heads = values.reshape(tok_rows, head_count, width)
    query_unit = unit_rows(query_heads)
    key_unit = unit_rows(key_heads)
    token_scale = float(total_tokens) ** (-0.5)
    cotangent = (
        -(learn_rates.T[:, :, None] * token_scale) * value_heads.astype(jnp.float32)
    ).astype(jnp.bfloat16)
    weight_rows = lax.all_gather(fast_weights.astype(jnp.bfloat16), "ctx", axis=2, tiled=True)
    gate = jnp.einsum(
        "thd,hrd->htr", key_unit, weight_rows[:, 0], preferred_element_type=jnp.float32
    )
    upward = jnp.einsum(
        "thd,hrd->htr", key_unit, weight_rows[:, 1], preferred_element_type=jnp.float32
    )
    back = jnp.einsum(
        "thd,hrd->htr", cotangent, weight_rows[:, 2], preferred_element_type=jnp.float32
    )
    sigma = jax.nn.sigmoid(gate)
    activated = jax.nn.silu(gate)
    hidden = (activated * upward).astype(jnp.bfloat16)
    gate_back = (back * upward * sigma * (1.0 + gate * (1.0 - sigma))).astype(jnp.bfloat16)
    up_back = (back * activated).astype(jnp.bfloat16)
    grad_gate = jnp.einsum("htr,thd->hrd", gate_back, key_unit, preferred_element_type=jnp.float32)
    grad_up = jnp.einsum("htr,thd->hrd", up_back, key_unit, preferred_element_type=jnp.float32)
    grad_down = jnp.einsum("htr,thd->hrd", hidden, cotangent, preferred_element_type=jnp.float32)
    gradient = jnp.stack([grad_gate, grad_up, grad_down], axis=1)
    share = lax.psum_scatter(
        gradient.astype(jnp.bfloat16), "ctx", scatter_dimension=2, tiled=True
    ).astype(jnp.float32)
    fast_updated = fast_weights - (momentum_decay * momentum + share)
    new_rows = lax.all_gather(fast_updated.astype(jnp.bfloat16), "ctx", axis=2, tiled=True)
    own_start = rep_index * per_rep
    partial_out = swiglu_apply(query_unit, new_rows)
    traded = lax.all_to_all(
        partial_out.astype(jnp.bfloat16), "rep", split_axis=0, concat_axis=0, tiled=True
    ).astype(partial_out.dtype)
    fast_out = jnp.sum(traded.reshape(rep_count, per_rep, tok_rows, width), axis=0)
    attend_query = lax.dynamic_slice_in_dim(query_heads, own_start, per_rep, 1)
    attend_key = lax.dynamic_slice_in_dim(key_heads, own_start, per_rep, 1)
    attend_value = lax.dynamic_slice_in_dim(value_heads, own_start, per_rep, 1)
    key_prior, value_prior = passed_along((attend_key, attend_value), "ctx", 1)
    attended = window_attention(
        attend_query, attend_key, attend_value, key_prior, value_prior, ctx_index == 0
    )
    combined = attended + jnp.transpose(fast_out, (1, 0, 2))
    layer_output = combined.astype(jnp.bfloat16).reshape(tok_rows, per_rep * width)
    return (layer_output, fast_updated)


def solution(mesh):
    return jax.shard_map(
        on_device,
        mesh=mesh,
        in_specs=(
            P(("groups", "ctx"), "head"),
            P(("groups", "ctx"), "head"),
            P(("groups", "ctx"), "head"),
            P("head", ("groups", "ctx")),
            P(("groups", "head"), None, ("ctx", "rep"), None),
            P(("groups", "head"), None, ("ctx", "rep"), None),
        ),
        out_specs=(
            P(("groups", "ctx"), ("head", "rep")),
            P(("groups", "head"), None, ("ctx", "rep"), None),
        ),
        check_vma=False,
    )
```

profile of v0, /device:TPU:0, one launch (start us, length us, event | category | flops | bytes accessed | tf_op | source)
XLA Modules:
  0.0 324.0 jit_solution(14371064781295452740)
XLA Ops:
  7.2 2.9 copy.69
  10.6 0.7 copy-done.5
  11.7 93.9 %all-gather.3.cloned.1.call-done = bf16[4,3,320,640]{3,2,0,1:T(8,128)(2,1)} async-done(((bf16[4,3,80,640]{3,2,0,1:T(8,128)(2,1)}), bf16[4,3,320,640]{3,2,0,1:T(8,128)(2,1)}) %all-gather.3.cloned.1.call-update) | async-done | bytes 4915216 | tf_op jit(solution)/shard_map/all_gather | solution.py:74
  105.7 2.0 fusion.6
  107.7 2.0 fusion.8
  109.7 0.6 fusion.10
  110.3 2.0 fusion.7
  112.3 0.7 fusion.9
  113.6 2.8 pad_maximum_fusion
  116.5 86.9 %reduce-scatter.2.cloned.1.call-done = bf16[4,3,80,640]{3,2,0,1:T(8,128)(2,1)} async-done(((bf16[4,3,320,640]{3,2,0,1:T(8,128)(2,1)}), bf16[4,3,80,640]{3,2,0,1:T(8,128)(2,1)}) %reduce-scatter.2.cloned.1.call-update) | async-done | bytes 1228816 | tf_op jit(solution)/shard_map/reduce_scatter | solution.py:93
  203.5 4.4 %fusion.88 = (bf16[4,3,80,640]{3,2,0,1:T(8,128)(2,1)}, f32[4,3,80,640]{3,2,0,1:T(8,128)}) fusion(bf16[4,3,80,640]{3,2,0,1:T(8,128)(2,1)} %reduce-scatter.2.cloned.1.call-done, f32[4,3,80,640]{3,2,1,0:T(8,128)} %param.11, f32[4,3,80,640]{3,2,1,0:T(8,128)S(1)} %copy-done), kind=kLoop, calls=%fused_computation.86 | loop fusion | flops 3072000 | bytes 9830400 | tf_op jit(solution)/shard_map/convert_element_type | solution.py:97
  208.1 4.1 %collective-permute-start.1 = (bf16[128,2,640]{2,0,1:T(8,128)(2,1)S(1)}, bf16[128,2,640]{2,0,1:T(8,128)(2,1)}, u32[]{:S(2)}, u32[]{:S(2)}) collective-permute-start(bf16[128,2,640]{2,0,1:T(8,128)(2,1)S(1)} %copy.61), channel_id=1, source_target_pairs={{0,4},{4,8},{8,12},{1,5},{5,9},{9,13},{2,6},{6,10},{10,14},{3,7},{... | collective-permute-start | bytes 983048 | tf_op jit(solution)/shard_map/ppermute | solution.py:13
  212.2 0.7 constant_dynamic-slice_fusion.1
  213.0 4.1 %collective-permute-start = (bf16[128,2,640]{0,2,1:T(8,128)(2,1)}, bf16[128,2,640]{0,2,1:T(8,128)(2,1)}, u32[]{:S(2)}, u32[]{:S(2)}) collective-permute-start(bf16[128,2,640]{0,2,1:T(8,128)(2,1)} %constant_dynamic-slice_fusion.1), channel_id=1, source_target_pairs={{0,4},{4,8},{8,12},{1,5},{5,9},{9,13},{2,6},{6,10},{10,14},{3,7},{... | collective-permute-start | bytes 983048 | tf_op jit(solution)/shard_map/ppermute | solution.py:13
  217.0 1.4 copy.34
  218.7 2.8 collective-permute-done.1
  221.5 1.5 fusion.90
  223.0 1.6 copy.51
  224.6 80.5 %all-gather.5.cloned.1.call-done = bf16[4,3,320,640]{3,2,0,1:T(8,128)(2,1)} async-done(((bf16[4,3,80,640]{3,2,0,1:T(8,128)(2,1)}), bf16[4,3,320,640]{3,2,0,1:T(8,128)(2,1)}) %all-gather.5.cloned.1.call-update) | async-done | bytes 4915216 | tf_op jit(solution)/shard_map/all_gather | solution.py:97
  305.1 2.0 fusion.5
  307.1 2.9 fusion.12
  310.0 4.3 %all_to_all.5 = bf16[4,128,640]{2,1,0:T(8,128)(2,1)S(1)} all-to-all(bf16[4,128,640]{2,1,0:T(8,128)(2,1)S(1)} %fusion.12), channel_id=1, replica_groups=mesh['groups'=2,'ctx'=4,'head'=2,'rep'=2] {'rep'}, dimensions={0} | all-to-all | bytes 1310720 | tf_op jit(solution)/shard_map/all_to_all | solution.py:100
  314.6 2.0 fusion.20
  316.6 0.9 copy.50
  (33 shorter events, 2.3 us)
Async XLA Ops:
  7.2 3.1 copy-start.4
  7.2 98.5 %all-gather.3.cloned.1.call-start = ((), (), s32[]{:S(2)}) async-start(), calls=%async_computation.2 | async-start | bytes 6144000 | tf_op jit(solution)/shard_map/all_gather | solution.py:74
  10.1 1.1 copy-start.5
  10.2 1.6 copy-start.6
  10.2 193.3 %reduce-scatter.2.cloned.1.call-start = ((), (), s32[]{:S(2)}) async-start(), calls=%async_computation.3 | async-start | bytes 6144000 | tf_op jit(solution)/shard_map/reduce_scatter | solution.py:93
  11.5 101.5 %copy-start.2 = (bf16[128,2560]{0,1:T(8,128)(2,1)}, bf16[128,2560]{0,1:T(8,128)(2,1)S(1)}, u32[]{:S(2)}) copy-start(bf16[128,2560]{0,1:T(8,128)(2,1)S(1)} %copy.33) | copy-start | bytes 1966084
  116.5 87.0 %copy-start = (f32[4,3,80,640]{3,2,1,0:T(8,128)S(1)}, f32[4,3,80,640]{3,2,1,0:T(8,128)}, u32[]{:S(2)}) copy-start(f32[4,3,80,640]{3,2,1,0:T(8,128)} %param.10) | copy-start | bytes 7372804
  116.5 188.6 %all-gather.5.cloned.1.call-start = ((), (), s32[]{:S(2)}) async-start(), calls=%async_computation.4 | async-start | bytes 6144000 | tf_op jit(solution)/shard_map/all_gather | solution.py:97
  207.8 4.4 %copy-start.3 = (bf16[128,2560]{0,1:T(8,128)(2,1)S(1)}, bf16[128,2560]{0,1:T(8,128)(2,1)}, u32[]{:S(2)}) copy-start(bf16[128,2560]{0,1:T(8,128)(2,1)} %copy-done.2) | copy-start | bytes 1966084
  208.1 13.4 %collective-permute-start.1 = (bf16[128,2,640]{2,0,1:T(8,128)(2,1)S(1)}, bf16[128,2,640]{2,0,1:T(8,128)(2,1)}, u32[]{:S(2)}, u32[]{:S(2)}) collective-permute-start(bf16[128,2,640]{2,0,1:T(8,128)(2,1)S(1)} %copy.61), channel_id=1, source_target_pairs={{0,4},{4,8},{8,12},{1,5},{5,9},{9,13},{2,6},{6,10},{10,14},{3,7},{... | collective-permute-start | bytes 983048 | tf_op jit(solution)/shard_map/ppermute | solution.py:13
  213.0 10.1 %copy-start.1 = (f32[4,3,80,640]{3,2,0,1:T(8,128)S(1)}, f32[4,3,80,640]{3,2,0,1:T(8,128)}, u32[]{:S(2)}) copy-start(f32[4,3,80,640]{3,2,0,1:T(8,128)} %get-tuple-element.27) | copy-start | bytes 7372804
  213.0 101.7 %collective-permute-start = (bf16[128,2,640]{0,2,1:T(8,128)(2,1)}, bf16[128,2,640]{0,2,1:T(8,128)(2,1)}, u32[]{:S(2)}, u32[]{:S(2)}) collective-permute-start(bf16[128,2,640]{0,2,1:T(8,128)(2,1)} %constant_dynamic-slice_fusion.1), channel_id=1, source_target_pairs={{0,4},{4,8},{8,12},{1,5},{5,9},{9,13},{2,6},{6,10},{10,14},{3,7},{... | collective-permute-start | bytes 983048 | tf_op jit(solution)/shard_map/ppermute | solution.py:13
Sparse Core Ops, SparseCore 0:
  10.3 95.3 all-gather.2
  116.6 86.8 reduce-scatter.1
  208.0 97.0 all-gather.4
where the time goes:
time: 325 us; the launch traced here: 324 us
  waiting for transfers between devices  264 us (81%)
  matrix products  16.3 us (5%)
  between operations  13.9 us (4%)
  local copies, waits for them, and re-layouts  9.4 us (3%)
  starting transfers between devices  8.31 us (3%)
  other arithmetic  7.58 us (2%)
  blocking collectives  4.26 us (1%)
    all_gather x1, waiting for transfers between devices, on_device(): lax.all_gather(fast_weights.astype(jnp.bfloat16), 'ctx', axis=2, tiled=True)  93.9 us
    reduce_scatter x1, waiting for transfers between devices, on_device(): lax.psum_scatter(gradient.astype(jnp.bfloat16), 'ctx', scatter_dimension=...  86.9 us
    all_gather x1, waiting for transfers between devices, on_device(): lax.all_gather(fast_updated.astype(jnp.bfloat16), 'ctx', axis=2, tiled=True)  80.5 us
    unnamed x21, local copies, waits for them, and re-layouts  8.4 us
    ppermute x2, starting transfers between devices, passed_along(): lax.ppermute(value, axis, [(source, source + steps) for source in range(i...  8.19 us
  transfers between devices with their start and end apart: 5, of which 4 were waited for; matrix products, arithmetic and copies ran while one was open for 4% of the time, Pallas kernels for 0%

commit v1 on v0

--- a/solution.py
+++ b/solution.py
@@ -1,6 +1,10 @@
+import functools
+
 import jax
 import jax.numpy as jnp
 from jax import lax
+from jax.experimental import pallas as pl
+from jax.experimental.pallas import tpu as pltpu
 from jax.sharding import PartitionSpec as P
 
 epsilon = 1e-06
@@ -113,9 +117,407 @@
     return (layer_output, fast_updated)
 
 
+def contract(left, right, left_dim, right_dim):
+    return lax.dot_general(
+        left, right, (((left_dim,), (right_dim,)), ((), ())), preferred_element_type=jnp.float32
+    )
+
+
+def fused_kernel(
+    n, mine, decay, token_scale,
+    q_hbm, k_hbm, v_hbm, lr_ref, fw_hbm, mom_hbm,
+    out_hbm, fast_hbm,
+    tok, lrs, fw, mom, weights, w_send, base_peer, base_send, grad, new_w, g_send, g_recv,
+    attn, part, sums_right, sums_left, out_v,
+    in_sem, tok_send, tok_recv, lr_send, lr_recv, pair_send, pair_recv, sum_send, sum_recv, out_sem,
+):
+    MESH = pl.DeviceIdType.MESH
+    z = lax.axis_index("ctx")
+    r = lax.axis_index("rep")
+    heads, _, rows, width = fw.shape
+    tokens = tok.shape[3]
+    has_left, has_right = z > 0, z < n - 1
+    own, other = r * mine, (1 - r) * mine
+
+    def load(c, h):
+        ref = (k_hbm, v_hbm, q_hbm)[c]
+        column = pl.multiple_of((own + h) * width, 128)
+        return pltpu.make_async_copy(ref.at[:, pl.ds(column, width)], tok.at[z, c, h], in_sem.at[c, h])
+
+    for c in range(3):
+        for h in range(mine):
+            load(c, h).start()
+    load_fw = pltpu.make_async_copy(fw_hbm, fw, in_sem.at[3, 0])
+    load_mom = pltpu.make_async_copy(mom_hbm, mom, in_sem.at[3, 1])
+    load_fw.start()
+    load_mom.start()
+    for i in range(heads):
+        lrs[z, i] = lr_ref[i : i + 1, :] * (-token_scale)
+
+    barrier = pltpu.get_barrier_semaphore()
+    pl.semaphore_signal(barrier, inc=1, device_id={"rep": 1 - r}, device_id_type=MESH)
+
+    @pl.when(has_left)
+    def _():
+        pl.semaphore_signal(barrier, inc=1, device_id={"ctx": z - 1}, device_id_type=MESH)
+
+    @pl.when(has_right)
+    def _():
+        pl.semaphore_signal(barrier, inc=1, device_id={"ctx": z + 1}, device_id_type=MESH)
+
+    pl.semaphore_wait(barrier, 1 + has_left.astype(jnp.int32) + has_right.astype(jnp.int32))
+
+    def tok_copy(b, c, h, way):
+        return pltpu.make_async_remote_copy(
+            src_ref=tok.at[b, c, h], dst_ref=tok.at[b, c, h],
+            send_sem=tok_send.at[way, b, c, h], recv_sem=tok_recv.at[b, c, h],
+            device_id={"ctx": z + 1 - 2 * way}, device_id_type=MESH,
+        )
+
+    def lr_copy(b, way):
+        return pltpu.make_async_remote_copy(
+            src_ref=lrs.at[b], dst_ref=lrs.at[b],
+            send_sem=lr_send.at[way, b], recv_sem=lr_recv.at[b],
+            device_id={"ctx": z + 1 - 2 * way}, device_id_type=MESH,
+        )
+
+    def pair_copy(which):
+        src, dst = (
+            (w_send, weights.at[:, :, pl.ds(rows, rows), :]),
+            (base_send, base_peer),
+            (g_send, g_recv),
+        )[which]
+        return pltpu.make_async_remote_copy(
+            src_ref=src, dst_ref=dst, send_sem=pair_send.at[which], recv_sem=pair_recv.at[which],
+            device_id={"rep": 1 - r}, device_id_type=MESH,
+        )
+
+    def sum_copy(b, h, way):
+        return pltpu.make_async_remote_copy(
+            src_ref=part.at[b, h], dst_ref=(sums_right, sums_left)[way].at[b, h],
+            send_sem=sum_send.at[b, h], recv_sem=sum_recv.at[way, b, h],
+            device_id={"ctx": z + 1 - 2 * way}, device_id_type=MESH,
+        )
+
+    open_way = (has_right, has_left)
+
+    def own_send(make):
+        for way in range(2):
+            pl.when(open_way[way])(lambda way=way: make(way).start())
+
+    own_send(lambda way: lr_copy(z, way))
+    for h in range(mine):
+        for c in range(2):
+            load(c, h).wait()
+            own_send(lambda way: tok_copy(z, c, h, way))
+    for h in range(mine):
+        load(2, h).wait()
+
+    def own_queries(step):
+        for way in range(2):
+            last = z if way == 0 else n - 1 - z
+
+            @pl.when(jnp.logical_and(step == last, open_way[way]))
+            def _(way=way):
+                for h in range(mine):
+                    tok_copy(z, 2, h, way).start()
+
+    own_queries(0)
+
+    load_fw.wait()
+    for h in range(mine):
+        for m in range(3):
+            w_send[h, m] = fw[other + h, m].astype(jnp.bfloat16)
+    pair_copy(0).start()
+    for h in range(mine):
+        for m in range(3):
+            weights[h, m, :rows] = fw[own + h, m].astype(jnp.bfloat16)
+    load_mom.wait()
+    for h in range(mine):
+        for m in range(3):
+            base_send[h, m] = fw[other + h, m] - decay * mom[other + h, m]
+    pair_copy(1).start()
+    pair_copy(0).wait_recv()
+
+    def grad_block(b, first):
+        @pl.loop(0, mine)
+        def _(h):
+            key = unit_rows(tok[b, 0, h])
+            value = tok[b, 1, h]
+            rate = lrs[b, own + h]
+            both = contract(weights[h, 0:2].reshape(4 * rows, width), key, 1, 1)
+            gate, upward = both[: 2 * rows], both[2 * rows :]
+            back = contract(weights[h, 2], value, 1, 1) * rate
+            sigma = jax.nn.sigmoid(gate)
+            activated = gate * sigma
+            hidden = (activated * upward * rate).astype(jnp.bfloat16)
+            gate_back = (back * upward * sigma * (1.0 + gate * (1.0 - sigma))).astype(jnp.bfloat16)
+            up_back = (back * activated).astype(jnp.bfloat16)
+            terms = (
+                contract(gate_back, key, 1, 0),
+                contract(up_back, key, 1, 0),
+                contract(hidden, value, 1, 0),
+            )
+            for m in range(3):
+                grad[h, m] = terms[m] if first else grad[h, m] + terms[m]
+
+    def attend(with_prior):
+        @pl.loop(0, mine)
+        def _(h):
+            query = tok[z, 2, h]
+            scale = width ** (-0.5)
+            scores = contract(query, tok[z, 0, h], 1, 1) * scale
+            peak = jnp.max(scores, axis=-1, keepdims=True)
+            if with_prior:
+                prior = contract(query, tok[z - 1, 0, h], 1, 1) * scale
+                peak = jnp.maximum(peak, jnp.max(prior, axis=-1, keepdims=True))
+                prior = jnp.exp(prior - peak)
+            scores = jnp.exp(scores - peak)
+            total = jnp.sum(scores, axis=-1, keepdims=True)
+            if with_prior:
+                total = total + jnp.sum(prior, axis=-1, keepdims=True)
+            result = contract((scores / total).astype(jnp.bfloat16), tok[z, 1, h], 1, 0)
+            if with_prior:
+                result = result + contract((prior / total).astype(jnp.bfloat16), tok[z - 1, 1, h], 1, 0)
+            attn[h] = result
+
+    def from_left(step):
+        return z - step >= 0
+
+    def from_right(step):
+        return z + step < n
+
+    grad_block(z, True)
+
+    @pl.when(z == 0)
+    def _():
+        attend(False)
+
+    def pass_on(step, pieces, with_lr):
+        arrives = (from_left(step), from_right(step))
+        for way in range(2):
+            b = z - step if way == 0 else z + step
+            if with_lr:
+                @pl.when(arrives[way])
+                def _(way=way, b=b):
+                    lr_copy(b, way).wait_recv()
+                    pl.when(open_way[way])(lambda: lr_copy(b, way).start())
+
+        for c, h in pieces:
+            for way in range(2):
+                b = z - step if way == 0 else z + step
+
+                @pl.when(arrives[way])
+                def _(way=way, b=b):
+                    tok_copy(b, c, h, way).wait_recv()
+                    pl.when(open_way[way])(lambda: tok_copy(b, c, h, way).start())
+
+    def keys_step(step, carry):
+        pass_on(step, [(c, h) for h in range(mine) for c in range(2)], True)
+        own_queries(step)
+
+        @pl.when(from_left(step))
+        def _():
+            grad_block(z - step, False)
+
+        @pl.when(from_right(step))
+        def _():
+            grad_block(z + step, False)
+
+        @pl.when(jnp.logical_and(step == 1, has_left))
+        def _():
+            attend(True)
+
+        return carry
+
+    lax.fori_loop(1, n, keys_step, 0)
+
+    pair_copy(1).wait_recv()
+    for h in range(mine):
+        for m in range(3):
+            fresh = fw[own + h, m] - (decay * mom[own + h, m] + grad[h, m, :rows])
+            fw[own + h, m] = fresh
+            new_w[h, m, :rows] = fresh.astype(jnp.bfloat16)
+            new_w[h, m, rows:] = (base_peer[h, m] - grad[h, m, rows:]).astype(jnp.bfloat16)
+            g_send[h, m] = grad[h, m, rows:].astype(jnp.bfloat16)
+    pair_copy(2).start()
+    store_own = pltpu.make_async_copy(
+        fw.at[pl.ds(own, mine)], fast_hbm.at[pl.ds(own, mine)], out_sem.at[0]
+    )
+    store_own.start()
+
+    def apply(b, h):
+        query = unit_rows(tok[b, 2, h])
+        gate = contract(query, new_w[h, 0], 1, 1)
+        upward = contract(query, new_w[h, 1], 1, 1)
+        hidden = (gate * jax.nn.sigmoid(gate) * upward).astype(jnp.bfloat16)
+        return contract(hidden, new_w[h, 2], 1, 0)
+
+    @pl.loop(0, mine)
+    def _(h):
+        attn[h] = attn[h] + apply(z, h)
+
+    def queries_step(step, carry):
+        pass_on(step, [(2, h) for h in range(mine)], False)
+        for way in range(2):
+            b = z - step if way == 1 else z + step
+            source_there = from_left(step) if way == 1 else from_right(step)
+            starts_here = jnp.logical_not(has_right if way == 1 else has_left)
+
+            @pl.when(source_there)
+            def _(b=b, way=way, starts_here=starts_here):
+                @pl.loop(0, mine)
+                def _(h):
+                    part[b, h] = apply(b, h).astype(jnp.bfloat16)
+                    pl.when(starts_here)(lambda: sum_copy(b, h, way).start())
+
+        return carry
+
+    lax.fori_loop(1, n, queries_step, 0)
+
+    near_left = 2 * z < n - 1
+
+    def merge_step(step, carry):
+        for h in range(mine):
+            for way, turn in ((0, near_left), (1, None), (0, jnp.logical_not(near_left))):
+                b = step if way == 0 else n - 1 - step
+                there = jnp.logical_and(b > z, has_left) if way == 0 else jnp.logical_and(b < z, has_right)
+
+                @pl.when(there if turn is None else jnp.logical_and(there, turn))
+                def _(b=b, way=way):
+                    sum_copy(b, h, way).wait_recv()
+                    arrived = (sums_right, sums_left)[way][b, h].astype(jnp.float32)
+                    part[b, h] = (part[b, h].astype(jnp.float32) + arrived).astype(jnp.bfloat16)
+                    sum_copy(b, h, way).start()
+
+        return carry
+
+    lax.fori_loop(1, n, merge_step, 0)
+
+    pair_copy(2).wait_recv()
+    for h in range(mine):
+        for m in range(3):
+            fw[other + h, m] = fw[other + h, m] - (
+                decay * mom[other + h, m] + g_recv[h, m].astype(jnp.float32)
+            )
+    store_other = pltpu.make_async_copy(
+        fw.at[pl.ds(other, mine)], fast_hbm.at[pl.ds(other, mine)], out_sem.at[1]
+    )
+    store_other.start()
+
+    for h in range(mine):
+        @pl.when(has_left)
+        def _():
+            sum_copy(z, h, 0).wait_recv()
+            attn[h] = attn[h] + sums_right[z, h].astype(jnp.float32)
+
+        @pl.when(has_right)
+        def _():
+            sum_copy(z, h, 1).wait_recv()
+            attn[h] = attn[h] + sums_left[z, h].astype(jnp.float32)
+
+        out_v[:, h * width : (h + 1) * width] = attn[h].astype(jnp.bfloat16)
+    store_out = pltpu.make_async_copy(out_v, out_hbm, out_sem.at[2])
+    store_out.start()
+
+    for way in range(2):
+        @pl.when(open_way[way])
+        def _(way=way):
+            lr_copy(z, way).wait_send()
+            for h in range(mine):
+                for c in range(3):
+                    tok_copy(z, c, h, way).wait_send()
+
+    def drain(step, carry):
+        for way in range(2):
+            b = z - step if way == 0 else z + step
+            arrives = from_left(step) if way == 0 else from_right(step)
+
+            @pl.when(jnp.logical_and(arrives, open_way[way]))
+            def _(way=way, b=b):
+                lr_copy(b, way).wait_send()
+                for h in range(mine):
+                    for c in range(3):
+                        tok_copy(b, c, h, way).wait_send()
+
+            @pl.when(arrives)
+            def _(way=way, b=b):
+                for h in range(mine):
+                    sum_copy(b, h, 1 - way).wait_send()
+
+        return carry
+
+    lax.fori_loop(1, n, drain, 0)
+    for which in range(3):
+        pair_copy(which).wait_send()
+    store_own.wait()
+    store_other.wait()
+    store_out.wait()
+
+
+def fused_device(queries, key_vectors, values, learn_rates, fast_weights, momentum):
+    n = lax.axis_size("ctx")
+    tokens = queries.shape[0]
+    heads, _, rows, width = fast_weights.shape
+    mine = heads // 2
+    bf16, f32 = jnp.bfloat16, jnp.float32
+    hbm = pl.BlockSpec(memory_space=pl.ANY)
+    dma = pltpu.SemaphoreType.DMA
+    vmem = pltpu.VMEM
+    return pl.pallas_call(
+        functools.partial(fused_kernel, n, mine, momentum_decay, float(tokens * n) ** (-0.5)),
+        out_shape=(
+            jax.ShapeDtypeStruct((tokens, mine * width), bf16),
+            jax.ShapeDtypeStruct(fast_weights.shape, f32),
+        ),
+        in_specs=[hbm, hbm, hbm, pl.BlockSpec(memory_space=pltpu.VMEM), hbm, hbm],
+        out_specs=(hbm, hbm),
+        scratch_shapes=[
+            vmem((n, 3, mine, tokens, width), bf16),
+            vmem((n, heads, 1, tokens), f32),
+            vmem(fast_weights.shape, f32),
+            vmem(fast_weights.shape, f32),
+            vmem((mine, 3, 2 * rows, width), bf16),
+            vmem((mine, 3, rows, width), bf16),
+            vmem((mine, 3, rows, width), f32),
+            vmem((mine, 3, rows, width), f32),
+            vmem((mine, 3, 2 * rows, width), f32),
+            vmem((mine, 3, 2 * rows, width), bf16),
+            vmem((mine, 3, rows, width), bf16),
+            vmem((mine, 3, rows, width), bf16),
+            vmem((mine, tokens, width), f32),
+            vmem((n, mine, tokens, width), bf16),
+            vmem((n, mine, tokens, width), bf16),
+            vmem((n, mine, tokens, width), bf16),
+            vmem((tokens, mine * width), bf16),
+            dma((4, max(mine, 2))),
+            dma((2, n, 3, mine)),
+            dma((n, 3, mine)),
+            dma((2, n)),
+            dma((n,)),
+            dma((3,)),
+            dma((3,)),
+            dma((n, mine)),
+            dma((2, n, mine)),
+            dma((3,)),
+        ],
+        compiler_params=pltpu.CompilerParams(
+            collective_id=0, has_side_effects=True, vmem_limit_bytes=56 * 1024 * 1024
+        ),
+    )(queries, key_vectors, values, learn_rates, fast_weights, momentum)
+
+
+def per_device(*operands):
+    queries, fast_weights = operands[0], operands[4]
+    heads, _, rows, width = fast_weights.shape
+    fits = lax.axis_size("rep") == 2 and heads % 2 == 0 and lax.axis_size("ctx") <= 4
+    aligned = rows % 16 == 0 and width % 128 == 0 and queries.shape[0] == 128
+    return (fused_device if fits and aligned else on_device)(*operands)
+
+
 def solution(mesh):
     return jax.shard_map(
-        on_device,
+        per_device,
         mesh=mesh,
         in_specs=(
             P(("groups", "ctx"), "head"),

time: 325 us -> 97.4 us (0.30)
  waiting for transfers between devices: 264 us -> 0 us
  Pallas kernels: 0 us -> 91.5 us
  matrix products: 16.3 us -> 0 us
  between operations: 13.9 us -> 0.64 us
  starting transfers between devices: 8.31 us -> 0 us
  other arithmetic: 7.58 us -> 0 us
  local copies, waits for them, and re-layouts: 9.4 us -> 5.01 us
  blocking collectives: 4.26 us -> 0 us
    all_gather x2 -> x0, waiting for transfers between devices: 174 us -> none  [the longest x1 93.9 us: on_device(): lax.all_gather(fast_weights.astype(jnp.bfloat16), 'ctx', axis=2, tiled=True)]
    pallas_call x0 -> x1, Pallas kernels: none -> 91.5 us  [fused_device(): pl.pallas_call(functools.partial(fused_kernel, n, mine, momentum_decay, f...]
    reduce_scatter x1 -> x0, waiting for transfers between devices: 86.9 us -> none  [on_device(): lax.psum_scatter(gradient.astype(jnp.bfloat16), 'ctx', scatter_dimension=...]
    dot_general x9 -> x0, matrix products: 14.8 us -> none  [the longest x1 2.91 us: swiglu_apply(): jnp.einsum('htr,hrd->htd', hidden, weights[:, 2], preferred_element_type=...]
    ppermute x2 -> x0, starting transfers between devices: 8.19 us -> none  [passed_along(): lax.ppermute(value, axis, [(source, source + steps) for source in range(i...]
    convert_element_type x1 -> x0, other arithmetic: 4.36 us -> none  [on_device(): fast_updated.astype(jnp.bfloat16)]
    all_to_all x1 -> x0, blocking collectives: 4.26 us -> none  [on_device(): lax.all_to_all(partial_out.astype(jnp.bfloat16), 'rep', split_axis=0, con...]
    unnamed x21 -> x2, local copies, waits for them, and re-layouts: 8.4 us -> 5.01 us
  transfers between devices with their start and end apart: 5 -> 0, of which waited for: 4 -> 0; matrix products, arithmetic and copies ran while one was open for 4% -> 0% of each run, Pallas kernels for 0% -> 0%
where the time goes in v1:
time: 97.4 us; the launch traced here: 97.2 us
  Pallas kernels  91.5 us (94%)
  local copies, waits for them, and re-layouts  5.01 us (5%)
    pallas_call x1, Pallas kernels, fused_device(): pl.pallas_call(functools.partial(fused_kernel, n, mine, momentum_decay, f...  91.5 us
    unnamed x2, local copies, waits for them, and re-layouts  5.01 us

profile of v1, /device:TPU:0, one launch (start us, length us, event | category | flops | bytes accessed | tf_op | source)
XLA Modules:
  0.0 97.2 jit_solution(11894801785056866763)
XLA Ops:
  0.6 91.5 %shard_map.77 = (bf16[128,1280]{1,0:T(8,128)(2,1)}, f32[4,3,80,640]{3,2,1,0:T(8,128)}) custom-call(bf16[128,2560]{1,0:T(8,128)(2,1)} %q_hbm.1, bf16[128,2560]{1,0:T(8,128)(2,1)} %k_hbm.1, bf16[128,2560]{1,0:T(8,128)(2,1)} %v_hbm.1, f32[4,128]{1,0:T(4,128)} %lr_ref.1, f32[4,3,80,640]{3,2,1,0:T(8,128)} %fw_hbm.1, f32[4,3,80,640]{3,2,1,0:T(8,128)} %mom_hbm.1), custom_call_target="tpu_custom_call" | custom-call | tf_op jit(solution)/shard_map/pallas_call | solution.py:467
  92.2 1.7 %copy.10 = bf16[128,1280]{1,0:T(8,128)(2,1)} copy(bf16[128,1280]{1,0:T(8,128)(2,1)} %get-tuple-element.4) | data formatting | bytes 655360
  93.9 3.3 %copy.11 = f32[4,3,80,640]{3,2,1,0:T(8,128)} copy(f32[4,3,80,640]{3,2,1,0:T(8,128)} %get-tuple-element.5) | data formatting | bytes 4915200

commit v2 on v1

--- a/solution.py
+++ b/solution.py
@@ -135,7 +135,8 @@
     z = lax.axis_index("ctx")
     r = lax.axis_index("rep")
     heads, _, rows, width = fw.shape
-    tokens = tok.shape[3]
+    piece = part.shape[2]
+    cuts = tok.shape[3] // piece
     has_left, has_right = z > 0, z < n - 1
     own, other = r * mine, (1 - r) * mine
 
@@ -358,18 +359,23 @@
         attn[h] = attn[h] + apply(z, h)
 
     def queries_step(step, carry):
-        pass_on(step, [(2, h) for h in range(mine)], False)
-        for way in range(2):
-            b = z - step if way == 1 else z + step
-            source_there = from_left(step) if way == 1 else from_right(step)
-            starts_here = jnp.logical_not(has_right if way == 1 else has_left)
-
-            @pl.when(source_there)
-            def _(b=b, way=way, starts_here=starts_here):
-                @pl.loop(0, mine)
-                def _(h):
-                    part[b, h] = apply(b, h).astype(jnp.bfloat16)
-                    pl.when(starts_here)(lambda: sum_copy(b, h, way).start())
+        for h in range(mine):
+            pass_on(step, [(2, h)], False)
+            for way in range(2):
+                b = z - step if way == 1 else z + step
+                source_there = from_left(step) if way == 1 else from_right(step)
+                starts_here = jnp.logical_not(has_right if way == 1 else has_left)
+
+                @pl.when(source_there)
+                def _(b=b, way=way, starts_here=starts_here):
+                    result = apply(b, h).astype(jnp.bfloat16)
+                    for half in range(cuts):
+                        part[b, cuts * h + half] = result[half * piece : (half + 1) * piece]
+
+                    @pl.when(starts_here)
+                    def _():
+                        for half in range(cuts):
+                            sum_copy(b, cuts * h + half, way).start()
 
         return carry
 
@@ -378,7 +384,7 @@
     near_left = 2 * z < n - 1
 
     def merge_step(step, carry):
-        for h in range(mine):
+        for h in range(cuts * mine):
             for way, turn in ((0, near_left), (1, None), (0, jnp.logical_not(near_left))):
                 b = step if way == 0 else n - 1 - step
                 there = jnp.logical_and(b > z, has_left) if way == 0 else jnp.logical_and(b < z, has_right)
@@ -405,18 +411,20 @@
     )
     store_other.start()
 
-    for h in range(mine):
+    for p in range(cuts * mine):
+        h, at = p // cuts, pl.ds(p % cuts * piece, piece)
+
         @pl.when(has_left)
         def _():
-            sum_copy(z, h, 0).wait_recv()
-            attn[h] = attn[h] + sums_right[z, h].astype(jnp.float32)
+            sum_copy(z, p, 0).wait_recv()
+            attn[h, at] = attn[h, at] + sums_right[z, p].astype(jnp.float32)
 
         @pl.when(has_right)
         def _():
-            sum_copy(z, h, 1).wait_recv()
-            attn[h] = attn[h] + sums_left[z, h].astype(jnp.float32)
-
-        out_v[:, h * width : (h + 1) * width] = attn[h].astype(jnp.bfloat16)
+            sum_copy(z, p, 1).wait_recv()
+            attn[h, at] = attn[h, at] + sums_left[z, p].astype(jnp.float32)
+
+        out_v[at, h * width : (h + 1) * width] = attn[h, at].astype(jnp.bfloat16)
     store_out = pltpu.make_async_copy(out_v, out_hbm, out_sem.at[2])
     store_out.start()
 
@@ -442,8 +450,8 @@
 
             @pl.when(arrives)
             def _(way=way, b=b):
-                for h in range(mine):
-                    sum_copy(b, h, 1 - way).wait_send()
+                for p in range(cuts * mine):
+                    sum_copy(b, p, 1 - way).wait_send()
 
         return carry
 
@@ -460,6 +468,7 @@
     tokens = queries.shape[0]
     heads, _, rows, width = fast_weights.shape
     mine = heads // 2
+    cuts = 2
     bf16, f32 = jnp.bfloat16, jnp.float32
     hbm = pl.BlockSpec(memory_space=pl.ANY)
     dma = pltpu.SemaphoreType.DMA
@@ -486,9 +495,9 @@
             vmem((mine, 3, rows, width), bf16),
             vmem((mine, 3, rows, width), bf16),
             vmem((mine, tokens, width), f32),
-            vmem((n, mine, tokens, width), bf16),
-            vmem((n, mine, tokens, width), bf16),
-            vmem((n, mine, tokens, width), bf16),
+            vmem((n, cuts * mine, tokens // cuts, width), bf16),
+            vmem((n, cuts * mine, tokens // cuts, width), bf16),
+            vmem((n, cuts * mine, tokens // cuts, width), bf16),
             vmem((tokens, mine * width), bf16),
             dma((4, max(mine, 2))),
             dma((2, n, 3, mine)),
@@ -497,8 +506,8 @@
             dma((n,)),
             dma((3,)),
             dma((3,)),
-            dma((n, mine)),
-            dma((2, n, mine)),
+            dma((n, cuts * mine)),
+            dma((2, n, cuts * mine)),
             dma((3,)),
         ],
         compiler_params=pltpu.CompilerParams(

time: 97.4 us -> 97.2 us (level)
  no operation moved by 1% of the time
where the time goes in v2:
time: 97.2 us; the launch traced here: 97 us
  Pallas kernels  91.3 us (94%)
  local copies, waits for them, and re-layouts  5.01 us (5%)
    pallas_call x1, Pallas kernels, fused_device(): pl.pallas_call(functools.partial(fused_kernel, n, mine, momentum_decay, f...  91.3 us
    unnamed x2, local copies, waits for them, and re-layouts  5.01 us

profile of v2, /device:TPU:0, one launch (start us, length us, event | category | flops | bytes accessed | tf_op | source)
XLA Modules:
  0.0 97.0 jit_solution(971370824694664150)
XLA Ops:
  0.6 91.3 %shard_map.77 = (bf16[128,1280]{1,0:T(8,128)(2,1)}, f32[4,3,80,640]{3,2,1,0:T(8,128)}) custom-call(bf16[128,2560]{1,0:T(8,128)(2,1)} %q_hbm.1, bf16[128,2560]{1,0:T(8,128)(2,1)} %k_hbm.1, bf16[128,2560]{1,0:T(8,128)(2,1)} %v_hbm.1, f32[4,128]{1,0:T(4,128)} %lr_ref.1, f32[4,3,80,640]{3,2,1,0:T(8,128)} %fw_hbm.1, f32[4,3,80,640]{3,2,1,0:T(8,128)} %mom_hbm.1), custom_call_target="tpu_custom_call" | custom-call | tf_op jit(solution)/shard_map/pallas_call | solution.py:476
  92.0 1.7 %copy.10 = bf16[128,1280]{1,0:T(8,128)(2,1)} copy(bf16[128,1280]{1,0:T(8,128)(2,1)} %get-tuple-element.4) | data formatting | bytes 655360
  93.7 3.3 %copy.11 = f32[4,3,80,640]{3,2,1,0:T(8,128)} copy(f32[4,3,80,640]{3,2,1,0:T(8,128)} %get-tuple-element.5) | data formatting | bytes 4915200

commit v3 on v2

--- a/solution.py
+++ b/solution.py
@@ -473,7 +473,7 @@
     hbm = pl.BlockSpec(memory_space=pl.ANY)
     dma = pltpu.SemaphoreType.DMA
     vmem = pltpu.VMEM
-    return pl.pallas_call(
+    results = pl.pallas_call(
         functools.partial(fused_kernel, n, mine, momentum_decay, float(tokens * n) ** (-0.5)),
         out_shape=(
             jax.ShapeDtypeStruct((tokens, mine * width), bf16),
@@ -514,6 +514,43 @@
             collective_id=0, has_side_effects=True, vmem_limit_bytes=56 * 1024 * 1024
         ),
     )(queries, key_vectors, values, learn_rates, fast_weights, momentum)
+    layer_output, fast_updated = results
+    return hand_over(layer_output, fast_updated)
+
+
+def hand_over_kernel(out_in, fast_in, out_ref, fast_ref, out_v, fast_v, sem):
+    count = fast_in.shape[0]
+    reads = [pltpu.make_async_copy(out_in, out_v, sem.at[0])]
+    writes = [pltpu.make_async_copy(out_v, out_ref, sem.at[0])]
+    for i in range(count):
+        reads.append(pltpu.make_async_copy(fast_in.at[i], fast_v.at[i], sem.at[1 + i]))
+        writes.append(pltpu.make_async_copy(fast_v.at[i], fast_ref.at[i], sem.at[1 + i]))
+    for read in reads:
+        read.start()
+    for read, write in zip(reads, writes):
+        read.wait()
+        write.start()
+    for write in writes:
+        write.wait()
+
+
+def hand_over(layer_output, fast_updated):
+    hbm = pl.BlockSpec(memory_space=pl.ANY)
+    return pl.pallas_call(
+        hand_over_kernel,
+        out_shape=(
+            jax.ShapeDtypeStruct(layer_output.shape, layer_output.dtype),
+            jax.ShapeDtypeStruct(fast_updated.shape, fast_updated.dtype),
+        ),
+        in_specs=[hbm, hbm],
+        out_specs=(hbm, hbm),
+        scratch_shapes=[
+            pltpu.VMEM(layer_output.shape, layer_output.dtype),
+            pltpu.VMEM(fast_updated.shape, fast_updated.dtype),
+            pltpu.SemaphoreType.DMA((1 + fast_updated.shape[0],)),
+        ],
+        compiler_params=pltpu.CompilerParams(vmem_limit_bytes=56 * 1024 * 1024),
+    )(layer_output, fast_updated)
 
 
 def per_device(*operands):

time: 97.2 us -> 94.8 us (0.975)
  local copies, waits for them, and re-layouts: 5.01 us -> 0 us
  Pallas kernels: 91.3 us -> 94 us
    unnamed x2 -> x0, local copies, waits for them, and re-layouts: 5.01 us -> none
    pallas_call x0 -> x1, Pallas kernels: none -> 2.65 us  [hand_over(): pl.pallas_call(hand_over_kernel, out_shape=(jax.ShapeDtypeStruct(layer_ou...]
where the time goes in v3:
time: 94.8 us; the launch traced here: 94.6 us
  Pallas kernels  94 us (99%)
    pallas_call x1, Pallas kernels, fused_device(): pl.pallas_call(functools.partial(fused_kernel, n, mine, momentum_decay, f...  91.3 us
    pallas_call x1, Pallas kernels, hand_over(): pl.pallas_call(hand_over_kernel, out_shape=(jax.ShapeDtypeStruct(layer_ou...  2.65 us

profile of v3, /device:TPU:0, one launch (start us, length us, event | category | flops | bytes accessed | tf_op | source)
XLA Modules:
  0.0 94.6 jit_solution(6532992639294579242)
XLA Ops:
  0.6 91.3 %shard_map.77 = (bf16[128,1280]{1,0:T(8,128)(2,1)}, f32[4,3,80,640]{3,2,1,0:T(8,128)}) custom-call(bf16[128,2560]{1,0:T(8,128)(2,1)} %q_hbm.1, bf16[128,2560]{1,0:T(8,128)(2,1)} %k_hbm.1, bf16[128,2560]{1,0:T(8,128)(2,1)} %v_hbm.1, f32[4,128]{1,0:T(4,128)} %lr_ref.1, f32[4,3,80,640]{3,2,1,0:T(8,128)} %fw_hbm.1, f32[4,3,80,640]{3,2,1,0:T(8,128)} %mom_hbm.1), custom_call_target="tpu_custom_call" | custom-call | tf_op jit(solution)/shard_map/pallas_call | solution.py:476
  92.0 2.6 %shard_map.78 = (bf16[128,1280]{1,0:T(8,128)(2,1)}, f32[4,3,80,640]{3,2,1,0:T(8,128)}) custom-call(bf16[128,1280]{1,0:T(8,128)(2,1)} %get-tuple-element.4.out_in, f32[4,3,80,640]{3,2,1,0:T(8,128)} %get-tuple-element.5.fast_in), custom_call_target="tpu_custom_call" | custom-call | tf_op jit(solution)/shard_map/pallas_call | solution.py:539

commit v4 on v3

--- a/solution.py
+++ b/solution.py
@@ -315,7 +315,6 @@
 
     def keys_step(step, carry):
         pass_on(step, [(c, h) for h in range(mine) for c in range(2)], True)
-        own_queries(step)
 
         @pl.when(from_left(step))
         def _():
@@ -358,38 +357,46 @@
     def _(h):
         attn[h] = attn[h] + apply(z, h)
 
+    near_left = 2 * z < n - 1
+
     def queries_step(step, carry):
         for h in range(mine):
-            pass_on(step, [(2, h)], False)
-            for way in range(2):
-                b = z - step if way == 1 else z + step
-                source_there = from_left(step) if way == 1 else from_right(step)
-                starts_here = jnp.logical_not(has_right if way == 1 else has_left)
-
-                @pl.when(source_there)
-                def _(b=b, way=way, starts_here=starts_here):
+            for way, when in ((0, near_left), (1, None), (0, jnp.logical_not(near_left))):
+                b = step if way == 0 else n - 1 - step
+                there = b < z if way == 0 else b > z
+
+                @pl.when(there if when is None else jnp.logical_and(there, when))
+                def _(b=b, way=way):
+                    tok_copy(b, 2, h, way).wait_recv()
+                    pl.when(open_way[way])(lambda: tok_copy(b, 2, h, way).start())
                     result = apply(b, h).astype(jnp.bfloat16)
                     for half in range(cuts):
                         part[b, cuts * h + half] = result[half * piece : (half + 1) * piece]
 
-                    @pl.when(starts_here)
+                    @pl.when(jnp.logical_not(open_way[way]))
                     def _():
                         for half in range(cuts):
-                            sum_copy(b, cuts * h + half, way).start()
+                            sum_copy(b, cuts * h + half, 1 - way).start()
+
+            for way in range(2):
+                last = z - 1 if way == 0 else n - 2 - z
+
+                @pl.when(jnp.logical_and(step == last, open_way[way]))
+                def _(way=way):
+                    tok_copy(z, 2, h, way).start()
 
         return carry
 
-    lax.fori_loop(1, n, queries_step, 0)
-
-    near_left = 2 * z < n - 1
-
-    def merge_step(step, carry):
+    lax.fori_loop(0, n - 1, queries_step, 0)
+
+    def merge_step(turn, carry):
+        step = n - turn
         for h in range(cuts * mine):
-            for way, turn in ((0, near_left), (1, None), (0, jnp.logical_not(near_left))):
+            for way, when in ((0, near_left), (1, None), (0, jnp.logical_not(near_left))):
                 b = step if way == 0 else n - 1 - step
                 there = jnp.logical_and(b > z, has_left) if way == 0 else jnp.logical_and(b < z, has_right)
 
-                @pl.when(there if turn is None else jnp.logical_and(there, turn))
+                @pl.when(there if when is None else jnp.logical_and(there, when))
                 def _(b=b, way=way):
                     sum_copy(b, h, way).wait_recv()
                     arrived = (sums_right, sums_left)[way][b, h].astype(jnp.float32)

time: 94.8 us -> 82 us (0.86)
  Pallas kernels: 94 us -> 81.1 us
    pallas_call x1, Pallas kernels: 91.3 us -> 78.5 us  [fused_device(): pl.pallas_call(functools.partial(fused_kernel, n, mine, momentum_decay, f...]
where the time goes in v4:
time: 82 us; the launch traced here: 81.8 us
  Pallas kernels  81.1 us (99%)
    pallas_call x1, Pallas kernels, fused_device(): pl.pallas_call(functools.partial(fused_kernel, n, mine, momentum_decay, f...  78.5 us
    pallas_call x1, Pallas kernels, hand_over(): pl.pallas_call(hand_over_kernel, out_shape=(jax.ShapeDtypeStruct(layer_ou...  2.65 us

profile of v4, /device:TPU:0, one launch (start us, length us, event | category | flops | bytes accessed | tf_op | source)
XLA Modules:
  0.0 81.8 jit_solution(15803424843991671513)
XLA Ops:
  0.6 78.5 %shard_map.77 = (bf16[128,1280]{1,0:T(8,128)(2,1)}, f32[4,3,80,640]{3,2,1,0:T(8,128)}) custom-call(bf16[128,2560]{1,0:T(8,128)(2,1)} %q_hbm.1, bf16[128,2560]{1,0:T(8,128)(2,1)} %k_hbm.1, bf16[128,2560]{1,0:T(8,128)(2,1)} %v_hbm.1, f32[4,128]{1,0:T(4,128)} %lr_ref.1, f32[4,3,80,640]{3,2,1,0:T(8,128)} %fw_hbm.1, f32[4,3,80,640]{3,2,1,0:T(8,128)} %mom_hbm.1), custom_call_target="tpu_custom_call" | custom-call | tf_op jit(solution)/shard_map/pallas_call | solution.py:483
  79.1 2.6 %shard_map.78 = (bf16[128,1280]{1,0:T(8,128)(2,1)}, f32[4,3,80,640]{3,2,1,0:T(8,128)}) custom-call(bf16[128,1280]{1,0:T(8,128)(2,1)} %get-tuple-element.4.out_in, f32[4,3,80,640]{3,2,1,0:T(8,128)} %get-tuple-element.5.fast_in), custom_call_target="tpu_custom_call" | custom-call | tf_op jit(solution)/shard_map/pallas_call | solution.py:546
